TPU v7x, 32 devices: a whole 2x2x4 slice. The times are simulated.
32 devices in a mesh: gx: 8 (over y, x, core), gy: 4 (over z).
Axes of the slice: x: 2, y: 2, z: 4, core: 2. Of those that a mesh axis runs over, the one named last changes fastest.
Arguments:
- sources: bfloat16 [8, 4, 8, 64, 256], P('gx', 'gy'), may hold values from -12 to 12
- geometry: bfloat16 [8, 4, 8, 4, 256], P('gx', 'gy'), may hold values from -0.5 to 0.5, as said below
- near_lists: int32 [8, 4, 8, 24], P('gx', 'gy'), may hold values from -1 to 255, as said below
- far_lists: int32 [8, 4, 4, 16], P('gx', 'gy'), may hold values from 0 to 7, as said below
- bases_in: bfloat16 [8, 4, 4, 32, 8, 256], P('gx', 'gy')
- bases_out: bfloat16 [8, 4, 4, 32, 8, 256], P('gx', 'gy'), may hold values from -0.25 to 0.25
- couplings: float32 [8, 4, 4, 32, 512], P('gx', 'gy')
Outputs:
- potential: float32 [8, 4, 8, 64, 256], P('gx', 'gy')
Inputs may be any that keep to these rules, and one draw needn't show every extreme that they name: `near_lists`: for each leaf the first c entries are live, c between 1 and 24 and equal to 24 on some leaves and to 1 on others; the first is the leaf itself, and every live entry names a leaf on a device whose gx and gy indices differ from the leaf's by at most one, in a slot that differs from the leaf's slot by at most one; the other entries are -1. `far_lists`: level 0 entries are below 4, levels 1 and 2 below 8, level 3 below 2. `geometry`: rows 0 to 2 lie in [-0.5, 0.5], row 3 about 0.006 to 0.04.
All inputs are finite; a program needn't handle non-finite values.
Results may differ from a plain program's by a relative error of at most 0.0029.
Values may be sent and summed in bfloat16 or wider, within the bound.
A program may use at most 64 MiB of HBM per device.

v0:
```python
import math
import jax
import jax.numpy as jnp
from jax import lax
from jax.sharding import PartitionSpec as P

FOUR_PI = 4.0 * math.pi


def from_partner(x, axis, stride):
    return lax.ppermute(x, axis, [(i, i ^ 1 << stride) for i in range(lax.axis_size(axis))])


def extended(block, sides, width):
    for axis, dim in sides:
        count = lax.axis_size(axis)
        forward = [(i, i + 1) for i in range(count - 1)]
        backward = [(target, source) for source, target in forward]
        low = lax.ppermute(
            lax.slice_in_dim(block, block.shape[dim] - width, None, axis=dim), axis, forward
        )
        high = lax.ppermute(lax.slice_in_dim(block, 0, width, axis=dim), axis, backward)
        block = jnp.concatenate([low, block, high], axis=dim)
    return block


def near_block(target_geo, target_center, source_geo, source_center, source_vals, weight):
    target_pos = target_geo[:, :3, :].astype(jnp.float32) + target_center[:, :, None]
    source_pos = source_geo[:, :3, :].astype(jnp.float32) + source_center[:, :, None]
    squared = jnp.zeros(
        (target_pos.shape[0], target_pos.shape[2], source_pos.shape[2]), jnp.float32
    )
    for component in range(3):
        offset = target_pos[:, component, :, None] - source_pos[:, component, None, :]
        squared = squared + offset * offset
    panel_area = source_geo[:, 3, :].astype(jnp.float32)[:, None, :]
    kernel = (
        weight[:, None, None] * panel_area / (FOUR_PI * jnp.sqrt(squared + panel_area))
    ).astype(jnp.bfloat16)
    return jnp.einsum("lij,lrj->lri", kernel, source_vals, preferred_element_type=jnp.float32)


def column_level_sums(first_term, second_term, third_term):
    first_sum = first_term
    for bit in range(2):
        first_sum = first_sum + from_partner(first_sum, "gy", bit)
    second_sum, third_sum = lax.psum((second_term, third_term), "gy")
    return (first_sum, second_sum, third_sum)


def coarse_total(values):
    for bit in range(2):
        values = values + from_partner(values, "gx", bit)
    return values


def body(sources, geometry, near_lists, far_lists, bases_in, bases_out, couplings):
    leaf_dev = sources.shape[2]
    rhs_cols = sources.shape[3]
    panels = sources.shape[4]
    slot_total = near_lists.shape[3]
    row_pos = lax.axis_index("gx")
    col_pos = lax.axis_index("gy")
    col_devs = lax.axis_size("gy")
    packed = jnp.concatenate([sources, geometry], axis=3)
    block = extended(packed, (("gx", 0), ("gy", 1)), 1)
    block = block.reshape((9 * leaf_dev,) + packed.shape[3:])
    lists = near_lists[0, 0]
    live = lists >= 0
    safe = jnp.maximum(lists, 0)
    device = safe // leaf_dev
    src_row = device // col_devs
    src_col = device % col_devs
    src_leaf = safe % leaf_dev
    local = ((src_row - row_pos + 1) * 3 + (src_col - col_pos + 1)) * leaf_dev + src_leaf
    local = jnp.where(live, local, 4 * leaf_dev)
    centers = jnp.stack([src_row, src_col, src_leaf], axis=-1).astype(jnp.float32)
    weights = live.astype(jnp.float32)
    own_leaf = jnp.arange(leaf_dev, dtype=jnp.int32)
    own_center = jnp.stack(
        [jnp.zeros_like(own_leaf) + row_pos, jnp.zeros_like(own_leaf) + col_pos, own_leaf], axis=-1
    ).astype(jnp.float32)
    target_geo = geometry[0, 0]
    start_total = jnp.zeros((leaf_dev, rhs_cols, panels), jnp.float32)

    def add_slot(slot, total):
        index = lax.dynamic_index_in_dim(local, slot, 1, keepdims=False)
        chosen = jnp.take(block, index, axis=0)
        center = lax.dynamic_index_in_dim(centers, slot, 1, keepdims=False)
        weight = lax.dynamic_index_in_dim(weights, slot, 1, keepdims=False)
        return total + near_block(
            target_geo, own_center, chosen[:, rhs_cols:], center, chosen[:, :rhs_cols], weight
        )

    near_field = lax.fori_loop(0, slot_total, add_slot, start_total)
    projection = jnp.einsum(
        "aqlp,lrp->aqr", bases_in[0, 0], sources[0, 0], preferred_element_type=jnp.float32
    )
    first_sum, second_sum, column_three = column_level_sums(
        projection[1], projection[2], projection[3]
    )
    column_table = lax.all_gather(projection[0][None], "gy", axis=0, tiled=True)
    third_sum = coarse_total(column_three)
    table_one, table_two, table_three = (
        lax.all_gather(first_sum[None], "gx", axis=0, tiled=True),
        lax.all_gather(second_sum[None], "gx", axis=0, tiled=True),
        lax.all_gather(third_sum[None], "gx", axis=0, tiled=True),
    )
    table_three = table_three[::4]
    tables = (column_table, table_one, table_two, table_three)
    far_ids = far_lists[0, 0]
    gathered = jnp.stack([jnp.take(tables[level], far_ids[level], axis=0) for level in range(4)])
    gathered = gathered.reshape(4, -1, rhs_cols)
    interaction = jnp.einsum(
        "aqk,akr->aqr", couplings[0, 0], gathered, precision=lax.Precision.HIGHEST
    )
    summed_one, summed_two, summed_column = column_level_sums(
        interaction[1], interaction[2], interaction[3]
    )
    summed_three = coarse_total(summed_column)
    target_sum = jnp.stack([interaction[0], summed_one, summed_two, summed_three]).astype(
        jnp.bfloat16
    )
    far_field = jnp.einsum(
        "aqr,aqlp->lrp", target_sum, bases_out[0, 0], preferred_element_type=jnp.float32
    )
    return (near_field + far_field).reshape(sources.shape)


def solution(mesh):
    in_specs = (
        P("gx", "gy", None, None, None),
        P("gx", "gy", None, None, None),
        P("gx", "gy", None, None),
        P("gx", "gy", None, None),
        P("gx", "gy", None, None, None, None),
        P("gx", "gy", None, None, None, None),
        P("gx", "gy", None, None, None),
    )
    out_specs = P("gx", "gy", None, None, None)
    return jax.shard_map(body, mesh=mesh, in_specs=in_specs, out_specs=out_specs, check_vma=False)
```

profile of v0, /device:TPU:0, one launch (start us, length us, event | category | flops | bytes accessed | tf_op | source)
XLA Modules:
  0.0 249.7 jit_solution(3222020537244776442)
XLA Ops:
  1.9 2.4 collective-permute-start
  7.0 20.1 %all-reduce.1 = (f32[32,64]{1,0:T(8,128)S(1)}, f32[1,32,64]{2,1,0:T(8,128)S(1)}) all-reduce(f32[32,64]{1,0:T(8,128)S(1)} %get-tuple-element.230, f32[1,32,64]{2,1,0:T(8,128)S(1)} %get-tuple-element.231), channel_id=1, replica_groups=mesh['gx'=8,'gy'=4] {'gy'}, use_global_device_ids=true, to_apply=%region_3.5 | all-reduce | flops 4096 | bytes 32768 | tf_op jit(solution)/shard_map/psum | solution.py:47
  30.3 13.1 %all_gather.12 = f32[4,32,64]{2,1,0:T(8,128)S(1)} all-gather(f32[1,32,64]{2,1,0:T(8,128)S(1)} %get-tuple-element.229), channel_id=1, replica_groups=mesh['gx'=8,'gy'=4] {'gy'}, dimensions={0}, use_global_device_ids=true | all-gather | bytes 40960 | tf_op jit(solution)/shard_map/all_gather | solution.py:102
  44.6 12.6 %all_gather.14 = f32[8,32,64]{2,1,0:T(8,128)S(1)} all-gather(f32[1,32,64]{2,1,0:T(8,128)S(1)} %get-tuple-element.208), channel_id=1, replica_groups=mesh['gx'=8,'gy'=4] {'gx'}, dimensions={0}, use_global_device_ids=true | all-gather | bytes 73728 | tf_op jit(solution)/shard_map/all_gather | solution.py:106
  59.2 2.5 collective-permute-done.7
  61.7 8.4 %all-gather.1 = f32[256,64]{1,0:T(8,128)S(1)} all-gather(f32[32,64]{1,0:T(8,128)S(1)} %add.271), channel_id=3, replica_groups=mesh['gx'=8,'gy'=4] {'gx'}, dimensions={0}, use_global_device_ids=true | all-gather | bytes 73728 | tf_op jit(solution)/shard_map/all_gather | solution.py:107
  70.8 9.2 %all-gather = f32[256,64]{1,0:T(8,128)S(1)} all-gather(f32[32,64]{1,0:T(8,128)S(1)} %add.268), channel_id=2, replica_groups=mesh['gx'=8,'gy'=4] {'gx'}, dimensions={0}, use_global_device_ids=true | all-gather | bytes 73728 | tf_op jit(solution)/shard_map/all_gather | solution.py:105
  86.1 2.7 %collective-permute-start.8 = (f32[32,64]{1,0:T(8,128)S(1)}, f32[32,64]{1,0:T(8,128)S(1)}, u32[]{:S(2)}, u32[]{:S(2)}) collective-permute-start(f32[32,64]{1,0:T(8,128)S(1)} %get-tuple-element.226), channel_id=1, source_target_pairs={{0,1},{1,0},{2,3},{3,2},{4,5},{5,4},{6,7},{7,6},{8,9},{9,8},{10,11... | collective-permute-start | bytes 24584 | tf_op jit(solution)/shard_map/ppermute | solution.py:11
  88.8 29.6 %all-reduce = (f32[32,64]{1,0:T(8,128)S(1)}, bf16[32,64]{1,0:T(8,128)(2,1)S(1)}) all-reduce(f32[32,64]{1,0:T(8,128)S(1)} %get-tuple-element.227, f32[32,64]{1,0:T(8,128)S(1)} %get-tuple-element.228), channel_id=1, replica_groups=mesh['gx'=8,'gy'=4] {'gy'}, use_global_device_ids=true, to_apply=%region_5.7 | all-reduce | flops 4096 | bytes 28672 | tf_op jit(solution)/shard_map/psum | solution.py:47
  120.3 3.1 %collective-permute-done.9 = f32[32,64]{1,0:T(8,128)S(1)} collective-permute-done((f32[32,64]{1,0:T(8,128)S(1)}, f32[32,64]{1,0:T(8,128)S(1)}, u32[]{:S(2)}, u32[]{:S(2)}) %collective-permute-start.9) | collective-permute-done | bytes 8224 | tf_op jit(solution)/shard_map/ppermute | solution.py:11
  125.7 122.9 %while.14 = (s32[]{:T(128)}, f32[8,64,256]{2,1,0:T(8,128)S(1)}, s32[8,24]{0,1:T(8,128)S(1)}, bf16[72,68,256]{2,1,0:T(8,128)(2,1)}, f32[8,24]{0,1:T(8,128)S(1)}, ...) while((s32[]{:T(128)}, f32[8,64,256]{2,1,0:T(8,128)S(1)}, ...), condition=%wide.region_1.2_spmd.clone, body=%wide.region_0.1_spmd.clone.sunk | while | flops 73833520 | bytes 2773931 | solution.py:95
  125.7 2.3 gather_fusion
  130.9 2.3 gather_fusion
  136.0 2.3 gather_fusion
  146.2 2.3 gather_fusion
  156.5 2.3 gather_fusion
  171.8 2.3 gather_fusion
  177.0 2.3 gather_fusion
  187.2 2.3 gather_fusion
  207.7 2.3 gather_fusion
  212.8 2.3 gather_fusion
  228.2 2.3 gather_fusion
  238.4 2.3 gather_fusion
  243.6 2.3 gather_fusion
  (454 shorter events, 113.5 us)
Async XLA Ops:
  0.0 248.7 %copy-start = (bf16[1,1,4,32,8,256]{5,4,3,2,1,0:T(8,128)(2,1)S(1)}, bf16[1,1,4,32,8,256]{5,4,3,2,1,0:T(8,128)(2,1)}, u32[]{:S(2)}) copy-start(bf16[1,1,4,32,8,256]{5,4,3,2,1,0:T(8,128)(2,1)} %param.16) | copy-start | bytes 1572868
  0.0 44.4 %copy-start.3 = (s32[1,1,8,24]{3,2,1,0:T(8,128)S(1)}, s32[1,1,8,24]{3,2,1,0:T(8,128)}, u32[]{:S(2)}) copy-start(s32[1,1,8,24]{3,2,1,0:T(8,128)} %param.13) | copy-start | bytes 2308
  1.9 79.6 %collective-permute-start = (bf16[1,1,8,68,256]{4,2,1,0,3:T(8,128)(2,1)S(1)}, bf16[1,1,8,68,256]{4,2,1,0,3:T(8,128)(2,1)S(1)}, u32[]{:S(2)}, u32[]{:S(2)}) collective-permute-start(bf16[1,1,8,68,256]{4,2,1,0,3:T(8,128)(2,1)S(1)} %copy_dynamic-update-slice_fusion.1), channel_id=1, source_target_pairs={{0,4},{4,8},{8,12},{12,16},{16,20},{20,24},{24,28},{1,5},{5,9},{9,... | collective-permute-start | bytes 835592 | tf_op jit(solution)/shard_map/ppermute | solution.py:19
  4.3 77.3 %collective-permute-start.1 = (bf16[1,1,8,68,256]{4,2,1,0,3:T(8,128)(2,1)S(1)}, bf16[1,1,8,68,256]{4,2,1,0,3:T(8,128)(2,1)S(1)}, u32[]{:S(2)}, u32[]{:S(2)}) collective-permute-start(bf16[1,1,8,68,256]{4,2,1,0,3:T(8,128)(2,1)S(1)} %copy_dynamic-update-slice_fusion.1), channel_id=1, source_target_pairs={{4,0},{8,4},{12,8},{16,12},{20,16},{24,20},{28,24},{5,1},{9,5},{13... | collective-permute-start | bytes 835592 | tf_op jit(solution)/shard_map/ppermute | solution.py:22
  27.1 30.7 %collective-permute-start.6 = (f32[32,64]{1,0:T(8,128)S(1)}, f32[32,64]{1,0:T(8,128)S(1)}, u32[]{:S(2)}, u32[]{:S(2)}) collective-permute-start(f32[32,64]{1,0:T(8,128)S(1)} %get-tuple-element.207), channel_id=1, source_target_pairs={{0,4},{4,0},{8,12},{12,8},{16,20},{20,16},{24,28},{28,24},{1,5},{5... | collective-permute-start | bytes 24584 | tf_op jit(solution)/shard_map/ppermute | solution.py:11
  27.2 31.3 %collective-permute-start.4 = (f32[32,64]{1,0:T(8,128)S(1)}, f32[32,64]{1,0:T(8,128)S(1)}, u32[]{:S(2)}, u32[]{:S(2)}) collective-permute-start(f32[32,64]{1,0:T(8,128)S(1)} %get-tuple-element.232), channel_id=1, source_target_pairs={{0,1},{1,0},{2,3},{3,2},{4,5},{5,4},{6,7},{7,6},{8,9},{9,8},{10,11... | collective-permute-start | bytes 24584 | tf_op jit(solution)/shard_map/ppermute | solution.py:11
  57.9 3.8 %collective-permute-start.7 = (f32[32,64]{1,0:T(8,128)S(1)}, f32[32,64]{1,0:T(8,128)S(1)}, u32[]{:S(2)}, u32[]{:S(2)}) collective-permute-start(f32[32,64]{1,0:T(8,128)S(1)} %add.270), channel_id=1, source_target_pairs={{0,8},{4,12},{8,0},{12,4},{16,24},{20,28},{24,16},{28,20},{1,9},{5... | collective-permute-start | bytes 24584 | tf_op jit(solution)/shard_map/ppermute | solution.py:11
  58.5 12.3 %collective-permute-start.5 = (f32[32,64]{1,0:T(8,128)S(1)}, f32[32,64]{1,0:T(8,128)S(1)}, u32[]{:S(2)}, u32[]{:S(2)}) collective-permute-start(f32[32,64]{1,0:T(8,128)S(1)} %fusion.54), channel_id=1, source_target_pairs={{0,2},{1,3},{2,0},{3,1},{4,6},{5,7},{6,4},{7,5},{8,10},{9,11},{10,... | collective-permute-start | bytes 24584 | tf_op jit(solution)/shard_map/ppermute | solution.py:11
  61.7 19.2 %copy-start.4 = (f32[1,1,4,32,512]{4,3,2,1,0:T(8,128)S(1)}, f32[1,1,4,32,512]{4,3,2,1,0:T(8,128)}, u32[]{:S(2)}) copy-start(f32[1,1,4,32,512]{4,3,2,1,0:T(8,128)} %param.17) | copy-start | bytes 786436
  80.9 38.2 %copy-start.2 = (bf16[1,1,8,4,256]{4,3,2,1,0:T(4,128)(2,1)S(1)}, bf16[1,1,8,4,256]{4,3,2,1,0:T(4,128)(2,1)}, u32[]{:S(2)}) copy-start(bf16[1,1,8,4,256]{4,3,2,1,0:T(4,128)(2,1)} %param.12) | copy-start | bytes 49156
  82.6 40.8 %collective-permute-start.2 = (bf16[3,1,8,68,256]{4,2,3,1,0:T(8,128)(2,1)}, bf16[3,1,8,68,256]{4,2,3,1,0:T(8,128)(2,1)S(1)}, u32[]{:S(2)}, u32[]{:S(2)}) collective-permute-start(bf16[3,1,8,68,256]{4,2,3,1,0:T(8,128)(2,1)} %copy.46), channel_id=1, source_target_pairs={{0,1},{1,2},{2,3},{4,5},{5,6},{6,7},{8,9},{9,10},{10,11},{12,13},{... | collective-permute-start | bytes 2506760 | tf_op jit(solution)/shard_map/ppermute | solution.py:19
  84.8 38.7 %collective-permute-start.3 = (bf16[3,1,8,68,256]{4,2,3,1,0:T(8,128)(2,1)}, bf16[3,1,8,68,256]{4,2,3,1,0:T(8,128)(2,1)S(1)}, u32[]{:S(2)}, u32[]{:S(2)}) collective-permute-start(bf16[3,1,8,68,256]{4,2,3,1,0:T(8,128)(2,1)} %copy.46), channel_id=1, source_target_pairs={{1,0},{2,1},{3,2},{5,4},{6,5},{7,6},{9,8},{10,9},{11,10},{13,12},{... | collective-permute-start | bytes 2506760 | tf_op jit(solution)/shard_map/ppermute | solution.py:22
  86.1 32.4 %collective-permute-start.8 = (f32[32,64]{1,0:T(8,128)S(1)}, f32[32,64]{1,0:T(8,128)S(1)}, u32[]{:S(2)}, u32[]{:S(2)}) collective-permute-start(f32[32,64]{1,0:T(8,128)S(1)} %get-tuple-element.226), channel_id=1, source_target_pairs={{0,1},{1,0},{2,3},{3,2},{4,5},{5,4},{6,7},{7,6},{8,9},{9,8},{10,11... | collective-permute-start | bytes 24584 | tf_op jit(solution)/shard_map/ppermute | solution.py:11
  118.4 1.2 collective-permute-start.10
  118.5 4.8 %collective-permute-start.9 = (f32[32,64]{1,0:T(8,128)S(1)}, f32[32,64]{1,0:T(8,128)S(1)}, u32[]{:S(2)}, u32[]{:S(2)}) collective-permute-start(f32[32,64]{1,0:T(8,128)S(1)} %fusion.55), channel_id=1, source_target_pairs={{0,2},{1,3},{2,0},{3,1},{4,6},{5,7},{6,4},{7,5},{8,10},{9,11},{10,... | collective-permute-start | bytes 24584 | tf_op jit(solution)/shard_map/ppermute | solution.py:11
  119.7 3.7 %collective-permute-start.11 = (f32[32,64]{1,0:T(8,128)S(1)}, f32[32,64]{1,0:T(8,128)S(1)}, u32[]{:S(2)}, u32[]{:S(2)}) collective-permute-start(f32[32,64]{1,0:T(8,128)S(1)} %add.275), channel_id=1, source_target_pairs={{0,8},{4,12},{8,0},{12,4},{16,24},{20,28},{24,16},{28,20},{1,9},{5... | collective-permute-start | bytes 24584 | tf_op jit(solution)/shard_map/ppermute | solution.py:11
  123.7 2.1 copy-start.1
where the time goes:
time: 251 us; the launch traced here: 250 us
  blocking collectives  93 us (37%)
  local copies, waits for them, and re-layouts  67.1 us (27%)
  matrix products  56.5 us (23%)
  starting transfers between devices  12.5 us (5%)
  other arithmetic  12.2 us (5%)
  waiting for transfers between devices  5.95 us (2%)
    gather x24, local copies, waits for them, and re-layouts, add_slot(): chosen = jnp.take(block, index, axis=0)  55.6 us
    dot_general x24, matrix products, near_block(): jnp.einsum('lij,lrj->lri', kernel, source_vals, preferred_element_type=jn...  53.5 us
    psum x2, blocking collectives, column_level_sums(): second_sum, third_sum = lax.psum((second_term, third_term), 'gy')  49.7 us
    all_gather x1, blocking collectives, body(): column_table = lax.all_gather(projection[0][None], 'gy', axis=0, tiled=True)  13.1 us
    all_gather x1, blocking collectives, body(): lax.all_gather(second_sum[None], 'gx', axis=0, tiled=True)  12.6 us
    all_gather x1, blocking collectives, body(): lax.all_gather(first_sum[None], 'gx', axis=0, tiled=True)  9.15 us
    all_gather x1, blocking collectives, body(): lax.all_gather(third_sum[None], 'gx', axis=0, tiled=True)  8.41 us
    ppermute x8, waiting for transfers between devices, from_partner(): lax.ppermute(x, axis, [(i, i ^ 1 << stride) for i in range(lax.axis_size(...  5.94 us
  transfers between devices with their start and end apart: 12, of which 3 were waited for; matrix products, arithmetic and copies ran while one was open for 3% of the time, Pallas kernels for 0%

commit v1 on v0

--- a/solution.py
+++ b/solution.py
@@ -5,6 +5,28 @@
 from jax.sharding import PartitionSpec as P
 
 FOUR_PI = 4.0 * math.pi
+
+
+def laid_out(blocks, dim):
+    blocks = jnp.moveaxis(blocks, 0, dim)
+    dims = blocks.shape
+    return blocks.reshape(*dims[:dim], dims[dim] * dims[dim + 1], *dims[dim + 2 :])
+
+
+def ring_gather(value, axis, dim):
+    peers = lax.axis_size(axis)
+    pairs = [(i, (i + 1) % peers) for i in range(peers)]
+    back = [(b, a) for a, b in pairs]
+    lower, upper = ([], [])
+    for step in range(peers - 1):
+        if step % 2 == 0:
+            lower.append(lax.ppermute(lower[-1] if lower else value, axis, pairs))
+        else:
+            upper.append(lax.ppermute(upper[-1] if upper else value, axis, back))
+    pieces = jnp.stack([*lower[::-1], value, *upper])
+    shift = lax.axis_index(axis) - len(lower)
+    pieces = pieces[(jnp.arange(peers) - shift) % peers]
+    return laid_out(pieces, dim)
 
 
 def from_partner(x, axis, stride):
@@ -102,7 +124,7 @@
     column_table = lax.all_gather(projection[0][None], "gy", axis=0, tiled=True)
     third_sum = coarse_total(column_three)
     table_one, table_two, table_three = (
-        lax.all_gather(first_sum[None], "gx", axis=0, tiled=True),
+        ring_gather(first_sum[None], "gx", 0),
         lax.all_gather(second_sum[None], "gx", axis=0, tiled=True),
         lax.all_gather(third_sum[None], "gx", axis=0, tiled=True),
     )

time: 251 us -> 252 us (level)
  blocking collectives: 93 us -> 77.9 us
  starting transfers between devices: 12.5 us -> 22.6 us
  waiting for transfers between devices: 5.95 us -> 10.9 us
    all_gather x1 -> x0, blocking collectives: 9.15 us -> none  [body(): lax.all_gather(first_sum[None], 'gx', axis=0, tiled=True)]
    ppermute x0 -> x7, starting transfers between devices: none -> 5.77 us  [the longest x3 5.7 us: ring_gather(): upper.append(lax.ppermute(upper[-1] if upper else value, axis, back))]
    ppermute x8, starting transfers between devices: 5.4 us -> 10.6 us  [from_partner(): lax.ppermute(x, axis, [(i, i ^ 1 << stride) for i in range(lax.axis_size(...]
    psum x2, blocking collectives: 49.7 us -> 46.2 us  [column_level_sums(): second_sum, third_sum = lax.psum((second_term, third_term), 'gy')]
    all_gather x1, blocking collectives: 12.6 us -> 9.24 us  [body(): lax.all_gather(second_sum[None], 'gx', axis=0, tiled=True)]
    ppermute x0 -> x7, waiting for transfers between devices: none -> 2.8 us  [the longest x3 2.79 us: ring_gather(): upper.append(lax.ppermute(upper[-1] if upper else value, axis, back))]
  transfers between devices with their start and end apart: 12 -> 19, of which waited for: 3 -> 6; matrix products, arithmetic and copies ran while one was open for 3% -> 4% of each run, Pallas kernels for 0% -> 0%
where the time goes in v1:
time: 252 us; the launch traced here: 251 us
  blocking collectives  77.9 us (31%)
  local copies, waits for them, and re-layouts  67.7 us (27%)
  matrix products  56.5 us (22%)
  starting transfers between devices  22.6 us (9%)
  other arithmetic  12.9 us (5%)
  waiting for transfers between devices  10.9 us (4%)
    gather x24, local copies, waits for them, and re-layouts, add_slot(): chosen = jnp.take(block, index, axis=0)  55.6 us
    dot_general x24, matrix products, near_block(): jnp.einsum('lij,lrj->lri', kernel, source_vals, preferred_element_type=jn...  53.5 us
    psum x2, blocking collectives, column_level_sums(): second_sum, third_sum = lax.psum((second_term, third_term), 'gy')  46.2 us
    all_gather x1, blocking collectives, body(): column_table = lax.all_gather(projection[0][None], 'gy', axis=0, tiled=True)  13.2 us
    ppermute x8, starting transfers between devices, from_partner(): lax.ppermute(x, axis, [(i, i ^ 1 << stride) for i in range(lax.axis_size(...  10.6 us
    all_gather x1, blocking collectives, body(): lax.all_gather(second_sum[None], 'gx', axis=0, tiled=True)  9.24 us
    all_gather x1, blocking collectives, body(): lax.all_gather(third_sum[None], 'gx', axis=0, tiled=True)  9.23 us
    ppermute x8, waiting for transfers between devices, from_partner(): lax.ppermute(x, axis, [(i, i ^ 1 << stride) for i in range(lax.axis_size(...  8.14 us
  transfers between devices with their start and end apart: 19, of which 6 were waited for; matrix products, arithmetic and copies ran while one was open for 4% of the time, Pallas kernels for 0%

profile of v1, /device:TPU:0, one launch (start us, length us, event | category | flops | bytes accessed | tf_op | source)
XLA Modules:
  0.0 251.0 jit_solution(10748454129882271893)
XLA Ops:
  1.9 2.4 collective-permute-start
  7.0 2.5 collective-permute-start.4
  9.4 18.1 %all-reduce.1 = (f32[32,64]{1,0:T(8,128)S(1)}, f32[1,32,64]{2,1,0:T(8,128)S(1)}) all-reduce(f32[32,64]{1,0:T(8,128)S(1)} %get-tuple-element.230, f32[1,32,64]{2,1,0:T(8,128)S(1)} %get-tuple-element.231), channel_id=1, replica_groups=mesh['gx'=8,'gy'=4] {'gy'}, use_global_device_ids=true, to_apply=%region_3.5 | all-reduce | flops 4096 | bytes 32768 | tf_op jit(solution)/shard_map/psum | solution.py:69
  32.2 4.1 %collective-permute-done.5 = f32[32,64]{1,0:T(8,128)S(1)} collective-permute-done((f32[32,64]{1,0:T(8,128)S(1)}, f32[32,64]{1,0:T(8,128)S(1)}, u32[]{:S(2)}, u32[]{:S(2)}) %collective-permute-start.5) | collective-permute-done | bytes 8224 | tf_op jit(solution)/shard_map/ppermute | solution.py:33
  36.3 13.2 %all_gather.9 = f32[4,32,64]{2,1,0:T(8,128)S(1)} all-gather(f32[1,32,64]{2,1,0:T(8,128)S(1)} %get-tuple-element.229), channel_id=1, replica_groups=mesh['gx'=8,'gy'=4] {'gy'}, dimensions={0}, use_global_device_ids=true | all-gather | bytes 40960 | tf_op jit(solution)/shard_map/all_gather | solution.py:124
  50.6 4.1 %collective-permute-start.14 = (f32[32,64]{1,0:T(8,128)S(1)}, f32[32,64]{1,0:T(8,128)S(1)}, u32[]{:S(2)}, u32[]{:S(2)}) collective-permute-start(f32[32,64]{1,0:T(8,128)S(1)} %add.296), channel_id=1, source_target_pairs={{0,8},{4,12},{8,0},{12,4},{16,24},{20,28},{24,16},{28,20},{1,9},{5... | collective-permute-start | bytes 24584 | tf_op jit(solution)/shard_map/ppermute | solution.py:33
  54.7 9.2 %all_gather.10 = f32[8,32,64]{2,1,0:T(8,128)S(1)} all-gather(f32[1,32,64]{2,1,0:T(8,128)S(1)} %get-tuple-element.208), channel_id=1, replica_groups=mesh['gx'=8,'gy'=4] {'gx'}, dimensions={0}, use_global_device_ids=true | all-gather | bytes 73728 | tf_op jit(solution)/shard_map/all_gather | solution.py:128
  66.0 9.2 %all-gather = f32[256,64]{1,0:T(8,128)S(1)} all-gather(f32[32,64]{1,0:T(8,128)S(1)} %add.297), channel_id=2, replica_groups=mesh['gx'=8,'gy'=4] {'gx'}, dimensions={0}, use_global_device_ids=true | all-gather | bytes 73728 | tf_op jit(solution)/shard_map/all_gather | solution.py:129
  78.8 2.8 %collective-permute-start.12 = (f32[1,32,64]{2,1,0:T(8,128)S(1)}, f32[1,32,64]{2,1,0:T(8,128)S(1)}, u32[]{:S(2)}, u32[]{:S(2)}) collective-permute-start(f32[1,32,64]{2,1,0:T(8,128)S(1)} %collective-permute-done.11), channel_id=1, source_target_pairs={{4,0},{8,4},{12,8},{16,12},{20,16},{24,20},{28,24},{0,28},{5,1},{9... | collective-permute-start | bytes 24584 | tf_op jit(solution)/shard_map/ppermute | solution.py:25
  88.9 2.7 %collective-permute-start.15 = (f32[32,64]{1,0:T(8,128)S(1)}, f32[32,64]{1,0:T(8,128)S(1)}, u32[]{:S(2)}, u32[]{:S(2)}) collective-permute-start(f32[32,64]{1,0:T(8,128)S(1)} %get-tuple-element.226), channel_id=1, source_target_pairs={{0,1},{1,0},{2,3},{3,2},{4,5},{5,4},{6,7},{7,6},{8,9},{9,8},{10,11... | collective-permute-start | bytes 24584 | tf_op jit(solution)/shard_map/ppermute | solution.py:33
  91.6 28.1 %all-reduce = (f32[32,64]{1,0:T(8,128)S(1)}, bf16[32,64]{1,0:T(8,128)(2,1)S(1)}) all-reduce(f32[32,64]{1,0:T(8,128)S(1)} %get-tuple-element.227, f32[32,64]{1,0:T(8,128)S(1)} %get-tuple-element.228), channel_id=1, replica_groups=mesh['gx'=8,'gy'=4] {'gy'}, use_global_device_ids=true, to_apply=%region_5.7 | all-reduce | flops 4096 | bytes 28672 | tf_op jit(solution)/shard_map/psum | solution.py:69
  121.0 3.6 %collective-permute-done.16 = f32[32,64]{1,0:T(8,128)S(1)} collective-permute-done((f32[32,64]{1,0:T(8,128)S(1)}, f32[32,64]{1,0:T(8,128)S(1)}, u32[]{:S(2)}, u32[]{:S(2)}) %collective-permute-start.16) | collective-permute-done | bytes 8224 | tf_op jit(solution)/shard_map/ppermute | solution.py:33
  127.0 122.9 %while.14 = (s32[]{:T(128)}, f32[8,64,256]{2,1,0:T(8,128)S(1)}, s32[8,24]{0,1:T(8,128)S(1)}, bf16[72,68,256]{2,1,0:T(8,128)(2,1)}, f32[8,24]{0,1:T(8,128)S(1)}, ...) while((s32[]{:T(128)}, f32[8,64,256]{2,1,0:T(8,128)S(1)}, ...), condition=%wide.region_1.2_spmd.clone, body=%wide.region_0.1_spmd.clone.sunk | while | flops 73833520 | bytes 2773931 | solution.py:117
  132.2 2.3 gather_fusion
  137.3 2.3 gather_fusion
  147.5 2.3 gather_fusion
  157.8 2.3 gather_fusion
  188.5 2.3 gather_fusion
  193.6 2.3 gather_fusion
  209.0 2.3 gather_fusion
  214.1 2.3 gather_fusion
  229.5 2.3 gather_fusion
  239.8 2.3 gather_fusion
  244.9 2.3 gather_fusion
  (476 shorter events, 123.1 us)
Async XLA Ops:
  0.0 250.0 %copy-start = (bf16[1,1,4,32,8,256]{5,4,3,2,1,0:T(8,128)(2,1)S(1)}, bf16[1,1,4,32,8,256]{5,4,3,2,1,0:T(8,128)(2,1)}, u32[]{:S(2)}) copy-start(bf16[1,1,4,32,8,256]{5,4,3,2,1,0:T(8,128)(2,1)} %param.16) | copy-start | bytes 1572868
  1.9 83.3 %collective-permute-start = (bf16[1,1,8,68,256]{4,2,1,0,3:T(8,128)(2,1)S(1)}, bf16[1,1,8,68,256]{4,2,1,0,3:T(8,128)(2,1)S(1)}, u32[]{:S(2)}, u32[]{:S(2)}) collective-permute-start(bf16[1,1,8,68,256]{4,2,1,0,3:T(8,128)(2,1)S(1)} %constant_dynamic-update-slice_fusion), channel_id=1, source_target_pairs={{0,4},{4,8},{8,12},{12,16},{16,20},{20,24},{24,28},{1,5},{5,9},{9,... | collective-permute-start | bytes 835592 | tf_op jit(solution)/shard_map/ppermute | solution.py:41
  4.3 80.9 %collective-permute-start.1 = (bf16[1,1,8,68,256]{4,2,1,0,3:T(8,128)(2,1)S(1)}, bf16[1,1,8,68,256]{4,2,1,0,3:T(8,128)(2,1)S(1)}, u32[]{:S(2)}, u32[]{:S(2)}) collective-permute-start(bf16[1,1,8,68,256]{4,2,1,0,3:T(8,128)(2,1)S(1)} %constant_dynamic-update-slice_fusion), channel_id=1, source_target_pairs={{4,0},{8,4},{12,8},{16,12},{20,16},{24,20},{28,24},{5,1},{9,5},{13... | collective-permute-start | bytes 835592 | tf_op jit(solution)/shard_map/ppermute | solution.py:44
  7.0 24.6 %collective-permute-start.4 = (f32[32,64]{1,0:T(8,128)S(1)}, f32[32,64]{1,0:T(8,128)S(1)}, u32[]{:S(2)}, u32[]{:S(2)}) collective-permute-start(f32[32,64]{1,0:T(8,128)S(1)} %get-tuple-element.232), channel_id=1, source_target_pairs={{0,1},{1,0},{2,3},{3,2},{4,5},{5,4},{6,7},{7,6},{8,9},{9,8},{10,11... | collective-permute-start | bytes 24584 | tf_op jit(solution)/shard_map/ppermute | solution.py:33
  27.6 23.0 %collective-permute-start.13 = (f32[32,64]{1,0:T(8,128)S(1)}, f32[32,64]{1,0:T(8,128)S(1)}, u32[]{:S(2)}, u32[]{:S(2)}) collective-permute-start(f32[32,64]{1,0:T(8,128)S(1)} %get-tuple-element.207), channel_id=1, source_target_pairs={{0,4},{4,0},{8,12},{12,8},{16,20},{20,16},{24,28},{28,24},{1,5},{5... | collective-permute-start | bytes 24584 | tf_op jit(solution)/shard_map/ppermute | solution.py:33
  31.6 4.7 %collective-permute-start.5 = (f32[32,64]{1,0:T(8,128)S(1)}, f32[32,64]{1,0:T(8,128)S(1)}, u32[]{:S(2)}, u32[]{:S(2)}) collective-permute-start(f32[32,64]{1,0:T(8,128)S(1)} %fusion.56), channel_id=1, source_target_pairs={{0,2},{1,3},{2,0},{3,1},{4,6},{5,7},{6,4},{7,5},{8,10},{9,11},{10,... | collective-permute-start | bytes 24584 | tf_op jit(solution)/shard_map/ppermute | solution.py:33
  36.3 18.3 %collective-permute-start.6 = (f32[1,32,64]{2,1,0:T(8,128)S(1)}, f32[1,32,64]{2,1,0:T(8,128)S(1)}, u32[]{:S(2)}, u32[]{:S(2)}) collective-permute-start(f32[1,32,64]{2,1,0:T(8,128)S(1)} %add_bitcast_fusion), channel_id=1, source_target_pairs={{0,4},{4,8},{8,12},{12,16},{16,20},{20,24},{24,28},{28,0},{1,5},{5... | collective-permute-start | bytes 24584 | tf_op jit(solution)/shard_map/ppermute | solution.py:23
  50.6 15.4 %collective-permute-start.14 = (f32[32,64]{1,0:T(8,128)S(1)}, f32[32,64]{1,0:T(8,128)S(1)}, u32[]{:S(2)}, u32[]{:S(2)}) collective-permute-start(f32[32,64]{1,0:T(8,128)S(1)} %add.296), channel_id=1, source_target_pairs={{0,8},{4,12},{8,0},{12,4},{16,24},{20,28},{24,16},{28,20},{1,9},{5... | collective-permute-start | bytes 24584 | tf_op jit(solution)/shard_map/ppermute | solution.py:33
  54.7 11.3 %collective-permute-start.7 = (f32[1,32,64]{2,1,0:T(8,128)S(1)}, f32[1,32,64]{2,1,0:T(8,128)S(1)}, u32[]{:S(2)}, u32[]{:S(2)}) collective-permute-start(f32[1,32,64]{2,1,0:T(8,128)S(1)} %collective-permute-done.6), channel_id=1, source_target_pairs={{0,4},{4,8},{8,12},{12,16},{16,20},{20,24},{24,28},{28,0},{1,5},{5... | collective-permute-start | bytes 24584 | tf_op jit(solution)/shard_map/ppermute | solution.py:23
  64.5 11.5 %collective-permute-start.10 = (f32[1,32,64]{2,1,0:T(8,128)S(1)}, f32[1,32,64]{2,1,0:T(8,128)S(1)}, u32[]{:S(2)}, u32[]{:S(2)}) collective-permute-start(f32[1,32,64]{2,1,0:T(8,128)S(1)} %add_bitcast_fusion), channel_id=1, source_target_pairs={{4,0},{8,4},{12,8},{16,12},{20,16},{24,20},{28,24},{0,28},{5,1},{9... | collective-permute-start | bytes 24584 | tf_op jit(solution)/shard_map/ppermute | solution.py:25
  65.9 11.5 %collective-permute-start.8 = (f32[1,32,64]{2,1,0:T(8,128)S(1)}, f32[1,32,64]{2,1,0:T(8,128)S(1)}, u32[]{:S(2)}, u32[]{:S(2)}) collective-permute-start(f32[1,32,64]{2,1,0:T(8,128)S(1)} %collective-permute-done.7), channel_id=1, source_target_pairs={{0,4},{4,8},{8,12},{12,16},{16,20},{20,24},{24,28},{28,0},{1,5},{5... | collective-permute-start | bytes 24584 | tf_op jit(solution)/shard_map/ppermute | solution.py:23
  75.2 9.3 %copy-start.3 = (f32[1,1,4,32,512]{4,3,2,1,0:T(8,128)S(1)}, f32[1,1,4,32,512]{4,3,2,1,0:T(8,128)}, u32[]{:S(2)}) copy-start(f32[1,1,4,32,512]{4,3,2,1,0:T(8,128)} %param.17) | copy-start | bytes 786436
  75.9 2.9 %collective-permute-start.11 = (f32[1,32,64]{2,1,0:T(8,128)S(1)}, f32[1,32,64]{2,1,0:T(8,128)S(1)}, u32[]{:S(2)}, u32[]{:S(2)}) collective-permute-start(f32[1,32,64]{2,1,0:T(8,128)S(1)} %collective-permute-done.10), channel_id=1, source_target_pairs={{4,0},{8,4},{12,8},{16,12},{20,16},{24,20},{28,24},{0,28},{5,1},{9... | collective-permute-start | bytes 24584 | tf_op jit(solution)/shard_map/ppermute | solution.py:25
  77.4 4.2 %collective-permute-start.9 = (f32[1,32,64]{2,1,0:T(8,128)S(1)}, f32[1,32,64]{2,1,0:T(8,128)S(1)}, u32[]{:S(2)}, u32[]{:S(2)}) collective-permute-start(f32[1,32,64]{2,1,0:T(8,128)S(1)} %collective-permute-done.8), channel_id=1, source_target_pairs={{0,4},{4,8},{8,12},{12,16},{16,20},{20,24},{24,28},{28,0},{1,5},{5... | collective-permute-start | bytes 24584 | tf_op jit(solution)/shard_map/ppermute | solution.py:23
  78.8 4.2 %collective-permute-start.12 = (f32[1,32,64]{2,1,0:T(8,128)S(1)}, f32[1,32,64]{2,1,0:T(8,128)S(1)}, u32[]{:S(2)}, u32[]{:S(2)}) collective-permute-start(f32[1,32,64]{2,1,0:T(8,128)S(1)} %collective-permute-done.11), channel_id=1, source_target_pairs={{4,0},{8,4},{12,8},{16,12},{20,16},{24,20},{28,24},{0,28},{5,1},{9... | collective-permute-start | bytes 24584 | tf_op jit(solution)/shard_map/ppermute | solution.py:25
  84.6 35.9 %copy-start.2 = (bf16[1,1,8,4,256]{4,3,2,1,0:T(4,128)(2,1)S(1)}, bf16[1,1,8,4,256]{4,3,2,1,0:T(4,128)(2,1)}, u32[]{:S(2)}) copy-start(bf16[1,1,8,4,256]{4,3,2,1,0:T(4,128)(2,1)} %param.12) | copy-start | bytes 49156
  86.3 38.5 %collective-permute-start.2 = (bf16[3,1,8,68,256]{4,2,3,1,0:T(8,128)(2,1)}, bf16[3,1,8,68,256]{4,2,3,1,0:T(8,128)(2,1)S(1)}, u32[]{:S(2)}, u32[]{:S(2)}) collective-permute-start(bf16[3,1,8,68,256]{4,2,3,1,0:T(8,128)(2,1)} %copy.46), channel_id=1, source_target_pairs={{0,1},{1,2},{2,3},{4,5},{5,6},{6,7},{8,9},{9,10},{10,11},{12,13},{... | collective-permute-start | bytes 2506760 | tf_op jit(solution)/shard_map/ppermute | solution.py:41
  87.6 37.1 %collective-permute-start.3 = (bf16[3,1,8,68,256]{4,2,3,1,0:T(8,128)(2,1)}, bf16[3,1,8,68,256]{4,2,3,1,0:T(8,128)(2,1)S(1)}, u32[]{:S(2)}, u32[]{:S(2)}) collective-permute-start(bf16[3,1,8,68,256]{4,2,3,1,0:T(8,128)(2,1)} %copy.46), channel_id=1, source_target_pairs={{1,0},{2,1},{3,2},{5,4},{6,5},{7,6},{9,8},{10,9},{11,10},{13,12},{... | collective-permute-start | bytes 2506760 | tf_op jit(solution)/shard_map/ppermute | solution.py:44
  88.9 30.9 %collective-permute-start.15 = (f32[32,64]{1,0:T(8,128)S(1)}, f32[32,64]{1,0:T(8,128)S(1)}, u32[]{:S(2)}, u32[]{:S(2)}) collective-permute-start(f32[32,64]{1,0:T(8,128)S(1)} %get-tuple-element.226), channel_id=1, source_target_pairs={{0,1},{1,0},{2,3},{3,2},{4,5},{5,4},{6,7},{7,6},{8,9},{9,8},{10,11... | collective-permute-start | bytes 24584 | tf_op jit(solution)/shard_map/ppermute | solution.py:33
  119.7 1.2 collective-permute-start.17
  119.8 4.7 %collective-permute-start.16 = (f32[32,64]{1,0:T(8,128)S(1)}, f32[32,64]{1,0:T(8,128)S(1)}, u32[]{:S(2)}, u32[]{:S(2)}) collective-permute-start(f32[32,64]{1,0:T(8,128)S(1)} %fusion.57), channel_id=1, source_target_pairs={{0,2},{1,3},{2,0},{3,1},{4,6},{5,7},{6,4},{7,5},{8,10},{9,11},{10,... | collective-permute-start | bytes 24584 | tf_op jit(solution)/shard_map/ppermute | solution.py:33
  121.0 3.7 %collective-permute-start.18 = (f32[32,64]{1,0:T(8,128)S(1)}, f32[32,64]{1,0:T(8,128)S(1)}, u32[]{:S(2)}, u32[]{:S(2)}) collective-permute-start(f32[32,64]{1,0:T(8,128)S(1)} %add.301), channel_id=1, source_target_pairs={{0,8},{4,12},{8,0},{12,4},{16,24},{20,28},{24,16},{28,20},{1,9},{5... | collective-permute-start | bytes 24584 | tf_op jit(solution)/shard_map/ppermute | solution.py:33
  125.0 2.0 copy-start.1
